TPU v7x, 256 devices: a whole 4x4x8 slice. The times are simulated.
256 devices in a mesh: vtx: 64 (over y_hi, z, x), feat: 4 (over y_lo, core).
Axes of the slice: x: 4, y: 4 (y_hi: 2, y_lo: 2; y = y_hi * 2 + y_lo), z: 8, core: 2. Of those that a mesh axis runs over, the one named last changes fastest.
Arguments:
- features: bfloat16 [16384, 128], P('vtx'), may hold values from -6 to 6
- weight: bfloat16 [128, 512], P(None, 'feat'), may hold values from -0.5 to 0.5
- bias: float32 [512], P('feat'), may hold values from -3 to 3
- cotangent: bfloat16 [16384, 512], P('vtx', 'feat'), may hold values from -6 to 6
- adj_tiles: bfloat16 [16384, 128, 128], P('vtx'), may hold values from 0 to 0.039794922
- tile_rows: int32 [4096, 4], P('vtx'), may hold values from 0 to 1
- tile_cols: int32 [4096, 4], P('vtx'), may hold values from 0 to 1
- tile_counts: int32 [4096], P('vtx'), may hold values from 0 to 4, as said below
Outputs:
- output: bfloat16 [16384, 512], P('vtx', 'feat')
- grad_features: bfloat16 [16384, 128], P('vtx', 'feat')
- grad_weight: float32 [128, 512], P(None, 'feat')
- grad_bias: float32 [512], P('feat')
Inputs may be any that keep to these rules, and one draw needn't show every extreme that they name: `tile_counts`: A pair's count is at most 4; every diagonal pair d * 64 + d holds exactly 4; counts are skewed over row blocks.
All inputs are finite; a program needn't handle non-finite values.
Results may differ from a plain program's by a relative error of at most 0.007.
Values may be sent and summed in bfloat16 or wider, within the bound.
A program may use at most 128 MiB of HBM per device.

v0:
```python
import jax
import jax.numpy as jnp
from jax import lax
from jax.sharding import PartitionSpec as P


def passed_along(value, axis, steps):
    count = lax.axis_size(axis)
    pairs = [(source, (source + steps) % count) for source in range(count)]
    return lax.ppermute(value, axis, pairs)


def activation(v):
    return jax.nn.gelu(v, approximate=True)


def tile_products(tiles_here, gather_idx, scatter_idx, count, block, transpose):
    row_tiles = block.shape[0]
    source = jnp.take(block, gather_idx, axis=0)
    if transpose:
        prod = jnp.einsum("kji,kjc->kic", tiles_here, source, preferred_element_type=jnp.float32)
    else:
        prod = jnp.einsum("kij,kjc->kic", tiles_here, source, preferred_element_type=jnp.float32)
    valid = (jnp.arange(tiles_here.shape[0], dtype=jnp.int32) < count).astype(jnp.float32)
    onehot = (scatter_idx[:, None] == jnp.arange(row_tiles, dtype=jnp.int32)[None, :]).astype(
        jnp.float32
    )
    onehot = onehot * valid[:, None]
    return jnp.einsum("kr,kic->ric", onehot, prod, precision=lax.Precision.HIGHEST)


def block_term(tiles_here, gather_idx, scatter_idx, count, block, transpose):
    return tile_products(tiles_here, gather_idx, scatter_idx, count, block, transpose)


def on_device(features, weight, bias, cotangent, adj_tiles, tile_rows, tile_cols, tile_counts):
    blocks = lax.axis_size("vtx")
    mine = lax.axis_index("vtx")
    rows_dev = features.shape[0]
    tile = adj_tiles.shape[1]
    slots = tile_rows.shape[1]
    row_tiles = rows_dev // tile
    width = weight.shape[1]
    tiles_four = adj_tiles.reshape(blocks, slots, tile, tile)
    shape_tiles = (row_tiles, tile, width)
    zeros_tiles = jnp.zeros(shape_tiles, jnp.float32)
    hidden = jnp.dot(features, weight, preferred_element_type=jnp.float32).astype(jnp.bfloat16)
    piece = lax.all_gather(hidden, "vtx", axis=0, tiled=True)
    count_blocks = piece.shape[0] // rows_dev

    def advance(offset, acc):
        block = lax.dynamic_slice_in_dim(piece, offset * rows_dev, rows_dev, 0).reshape(shape_tiles)
        return acc + block_term(
            tiles_four[offset],
            tile_cols[offset],
            tile_rows[offset],
            tile_counts[offset],
            block,
            False,
        )

    aggregate = lax.fori_loop(0, count_blocks, advance, zeros_tiles)
    pre = aggregate.reshape(rows_dev, width) + bias
    result, pullback = jax.vjp(activation, pre)
    output = result.astype(jnp.bfloat16)
    grad_pre = pullback(cotangent.astype(jnp.float32))[0].astype(jnp.bfloat16)
    grad_tiles = grad_pre.reshape(shape_tiles)

    def own_term(target):
        return block_term(
            tiles_four[target],
            tile_rows[target],
            tile_cols[target],
            tile_counts[target],
            grad_tiles,
            True,
        )

    def turn(step, acc):
        target = (mine + 1 + step) % blocks
        acc = acc + own_term(target)
        return passed_along(acc, "vtx", -1)

    carried = lax.fori_loop(0, blocks - 1, turn, zeros_tiles)
    grad_hidden = (carried + own_term(mine)).reshape(rows_dev, width)
    grad_round = grad_hidden.astype(jnp.bfloat16)
    local_weight = jnp.einsum("rf,rc->fc", features, grad_round, preferred_element_type=jnp.float32)
    local_bias = jnp.sum(grad_pre.astype(jnp.float32), axis=0)
    grad_weight, grad_bias = lax.psum((local_weight, local_bias), "vtx")
    partial_inputs = jnp.einsum("rc,fc->rf", grad_round, weight, preferred_element_type=jnp.float32)
    grad_features = lax.psum_scatter(
        partial_inputs, "feat", scatter_dimension=1, tiled=True
    ).astype(jnp.bfloat16)
    return (output, grad_features, grad_weight, grad_bias)


def solution(mesh):
    in_specs = (
        P("vtx", None),
        P(None, "feat"),
        P("feat"),
        P("vtx", "feat"),
        P("vtx", None, None),
        P("vtx", None),
        P("vtx", None),
        P("vtx"),
    )
    out_specs = (P("vtx", "feat"), P("vtx", "feat"), P(None, "feat"), P("feat"))
    return jax.shard_map(
        on_device, mesh=mesh, in_specs=in_specs, out_specs=out_specs, check_vma=False
    )
```

profile of v0, /device:TPU:2, one launch (start us, length us, event | category | flops | bytes accessed | tf_op | source)
XLA Modules:
  0.0 2078.9 jit_solution(10331711519618311670)
XLA Ops:
  14.0 129.1 %all-gather.2.cloned.1.call-done = bf16[16384,128]{1,0:T(8,128)(2,1)} async-done(((bf16[256,128]{1,0:T(8,128)(2,1)}), bf16[16384,128]{1,0:T(8,128)(2,1)}) %all-gather.2.cloned.1.call-update) | async-done | bytes 4194320 | tf_op jit(solution)/shard_map/all_gather | solution.py:48
  143.1 349.0 %while.30 = (s32[]{:T(128)}, f32[2,128,128]{2,0,1:T(2,128)S(1)}, s32[64,4]{1,0:T(8,128)S(1)}, s32[64]{0:T(128)}, bf16[64,4,128,128]{3,2,1,0:T(8,128)(2,1)}, /*in...) while((s32[]{:T(128)}, f32[2,128,128]{2,0,1:T(2,128)S(1)}, ...), condition=%wide.region_1.3_spmd.clone, body=%wide.region_0.2_spmd.clone.sunk | while | flops 18482228 | bytes 1446245 | solution.py:62
  495.5 950.0 %while.29 = (s32[]{:T(128)}, f32[2,128,128]{2,0,1:T(2,128)S(1)}, s32[]{:T(128)}, s32[64,4]{1,0:T(8,128)S(1)}, s32[64]{0:T(128)}, /*index=5*/bf16[64,4,128,128]{3...) while((s32[]{:T(128)}, f32[2,128,128]{2,0,1:T(2,128)S(1)}, ...), condition=%wide.region_3.5_spmd, body=%wide.region_2.4_spmd.sunk | while | flops 18449472 | bytes 1839596 | solution.py:84
  533.2 8.3 collective-permute-start
  548.3 8.3 collective-permute-start
  563.5 8.3 collective-permute-start
  578.6 8.3 collective-permute-start
  593.8 8.3 collective-permute-start
  624.6 8.6 collective-permute-start
  656.0 8.3 collective-permute-start
  716.7 8.3 collective-permute-start
  762.2 8.3 collective-permute-start
  807.6 8.5 collective-permute-start
  824.2 8.5 collective-permute-start
  840.0 8.3 collective-permute-start
  855.2 8.3 collective-permute-start
  900.7 8.3 collective-permute-start
  961.4 8.3 collective-permute-start
  1007.2 8.6 collective-permute-start
  1038.9 8.3 collective-permute-start
  1054.1 8.3 collective-permute-start
  1099.6 8.3 collective-permute-start
  1145.0 8.3 collective-permute-start
  1206.5 8.5 collective-permute-start
  1237.6 8.3 collective-permute-start
  1283.1 8.3 collective-permute-start
  1343.7 8.3 collective-permute-start
  1389.2 8.3 collective-permute-start
  1404.4 8.3 collective-permute-start
  1448.0 185.6 %psum.15 = f32[128]{0:T(128)} all-reduce(f32[128]{0:T(128)S(1)} %get-tuple-element.428), channel_id=1, replica_groups=mesh['vtx'=64,'feat'=4] {'vtx'}, use_global_device_ids=true, to_apply=%region_7.9 | all-reduce | flops 128 | bytes 1024 | tf_op jit(solution)/shard_map/psum | solution.py:89
  1633.6 417.9 %all-reduce.2.cloned.1.call-done = f32[128,128]{0,1:T(8,128)} async-done(((f32[128,128]{0,1:T(8,128)}), f32[128,128]{0,1:T(8,128)}) %all-reduce.2.cloned.1.call-update) | async-done | bytes 65552 | tf_op jit(solution)/shard_map/psum | solution.py:89
  2053.0 18.0 reduce-scatter.2.cloned.1.call-done
  (1211 shorter events, 1091.1 us)
Async XLA Ops:
  7.2 135.9 %all-gather.2.cloned.1.call-start = ((), (), s32[]{:S(2)}) async-start(), calls=%async_computation.1 | async-start | bytes 4259840 | tf_op jit(solution)/shard_map/all_gather | solution.py:48
  9.6 2041.9 %all-reduce.2.cloned.1.call-start = ((), (), s32[]{:S(2)}) async-start(), calls=%async_computation.3 | async-start | bytes 131072 | tf_op jit(solution)/shard_map/psum | solution.py:89
  533.2 10.8 collective-permute-start
  578.6 10.8 collective-permute-start
  593.8 10.8 collective-permute-start
  608.9 11.2 collective-permute-start
  624.6 12.2 collective-permute-start
  656.0 10.8 collective-permute-start
  716.7 10.8 collective-permute-start
  731.9 10.8 collective-permute-start
  762.2 10.8 collective-permute-start
  777.3 10.8 collective-permute-start
  807.6 12.2 collective-permute-start
  824.2 11.4 collective-permute-start
  840.0 10.8 collective-permute-start
  855.2 10.8 collective-permute-start
  870.4 10.8 collective-permute-start
  900.7 10.8 collective-permute-start
  915.9 10.8 collective-permute-start
  961.4 10.8 collective-permute-start
  991.7 11.1 collective-permute-start
  1007.2 12.3 collective-permute-start
  1038.9 10.8 collective-permute-start
  1054.1 10.8 collective-permute-start
  1190.5 11.6 collective-permute-start
  1206.5 11.9 collective-permute-start
  1237.6 10.8 collective-permute-start
  1374.1 10.8 collective-permute-start
  1389.2 10.8 collective-permute-start
  1404.4 10.8 collective-permute-start
  1419.6 10.8 collective-permute-start
  1447.1 623.9 %reduce-scatter.2.cloned.1.call-start = ((), (), s32[]{:S(2)}) async-start(), calls=%async_computation.2 | async-start | bytes 163840 | tf_op jit(solution)/shard_map/reduce_scatter | solution.py:91
  (36 other events, 1658.3 us)
Sparse Core Ops, SparseCore 0:
  12.2 130.8 all-gather.1
  1447.2 604.1 all-reduce.1
  2054.1 16.8 reduce-scatter.1
where the time goes:
time: 2090 us; the launch traced here: 2080 us
  waiting for transfers between devices  733 us (35%)
  starting transfers between devices  506 us (24%)
  local copies, waits for them, and re-layouts  293 us (14%)
  matrix products  252 us (12%)
  blocking collectives  186 us (9%)
  other arithmetic  87.9 us (4%)
    ppermute x63, starting transfers between devices, passed_along(): return lax.ppermute(value, axis, pairs)  506 us
    psum x1, waiting for transfers between devices, on_device(): grad_weight, grad_bias = lax.psum((local_weight, local_bias), 'vtx')  418 us
    psum x1, blocking collectives, on_device(): grad_weight, grad_bias = lax.psum((local_weight, local_bias), 'vtx')  186 us
    ppermute x63, waiting for transfers between devices, passed_along(): return lax.ppermute(value, axis, pairs)  168 us
    all_gather x1, waiting for transfers between devices, on_device(): piece = lax.all_gather(hidden, 'vtx', axis=0, tiled=True)  129 us
    dot_general x128, matrix products, tile_products(): jnp.einsum('kr,kic->ric', onehot, prod, precision=lax.Precision.HIGHEST)  101 us
    convert_element_type x128, other arithmetic, tile_products(): (jnp.arange(tiles_here.shape[0], dtype=jnp.int32) < count).astype(jnp.flo...  82.8 us
    dynamic_slice x64, local copies, waits for them, and re-layouts, own_term(): tile_counts[target]  79.6 us
  transfers between devices with their start and end apart: 66, of which 66 were waited for; matrix products, arithmetic and copies ran while one was open for 0% of the time, Pallas kernels for 0%

commit v1 on v0

v1 whole, which is shorter than its diff:
```python
import functools
import math

import jax
import jax.numpy as jnp
from jax import lax
from jax.experimental import pallas as pl
from jax.experimental.pallas import tpu as pltpu
from jax.sharding import PartitionSpec as P

MESH = pl.DeviceIdType.MESH
RING_X = 4
T = 128
SLOTS = 4
F32 = jnp.float32
BF16 = jnp.bfloat16


def dot(a, b, dims=((1,), (0,))):
    return lax.dot_general(a, b, (dims, ((), ())), preferred_element_type=F32)


def split(v):
    high = v.astype(BF16)
    return high, (v - high.astype(F32)).astype(BF16)


def gelu_parts(v):
    c = math.sqrt(2.0 / math.pi)
    t = jnp.tanh(c * (v + 0.044715 * (v * v * v)))
    cdf = 0.5 * (1.0 + t)
    slope = cdf + 0.5 * v * (1.0 - t * t) * (c * (1.0 + (3.0 * 0.044715) * (v * v)))
    return v * cdf, slope


def kernel(
    Z,
    feat_h,
    weight_h,
    bias_h,
    cot_h,
    tiles_h,
    rows,
    cols,
    counts,
    out_ref,
    gf_ref,
    gw_ref,
    gb_ref,
    xg,
    tiles,
    w,
    bias,
    cot,
    acc,
    ex,
    sb,
    axf,
    gp,
    pt,
    pe,
    pb,
    pf,
    gwb,
    g1,
    g2s,
    g2,
    g3,
    sbuf,
    rbuf,
    fs,
    fr,
    lsem,
    ssem,
    rsem,
    exs,
    exr,
    gsem,
    g1r,
    g2r,
    g3r,
    tsem,
    trsem,
    fsem,
    frsem,
):
    X = RING_X
    H = Z // 2
    R = T // Z
    me_v = lax.axis_index("vtx")
    me_f = lax.axis_index("feat")
    h = me_v // (Z * X)
    z = (me_v // X) % Z
    x = me_v % X
    l = me_f // 2
    c = me_f % 2

    def vid(hh, zz, xx):
        return (hh * Z + zz) * X + xx

    def here(zz, xx):
        return (vid(h, zz, xx), me_f)

    core_mate = (me_v, l * 2 + 1 - c)
    lo_mate = (me_v, (1 - l) * 2 + c)
    swap_mate = (vid(1 - h, z, x), (1 - l) * 2 + c)

    def zat(o):
        return (z + Z + o) % Z

    def xat(o):
        return (x + X + o) % X

    def sgn(i):
        return 1 - 2 * (i % 2)

    def off(q):
        return ((q + 1) // 2) * (1 - 2 * (q % 2))

    p0 = z * X + x

    half_rows = pl.ds(pl.multiple_of(c * T, T), T)
    n_half = Z * X
    tiles_copy = pltpu.make_async_copy(
        tiles_h.at[pl.ds(l * (n_half * SLOTS), n_half * SLOTS)], tiles, lsem.at[0]
    )
    w_copy = pltpu.make_async_copy(weight_h, w, lsem.at[1])
    bias_copy = pltpu.make_async_copy(bias_h, bias, lsem.at[2])
    cot_copy = pltpu.make_async_copy(cot_h, cot, lsem.at[3])
    own_copy = pltpu.make_async_copy(feat_h.at[half_rows], xg.at[p0], lsem.at[4])

    @pl.when(h == l)
    def _():
        own_copy.start()

    tiles_copy.start()
    w_copy.start()
    bias_copy.start()
    cot_copy.start()

    barrier = pltpu.get_barrier_semaphore()

    def greet(v, f):
        pl.semaphore_signal(barrier, inc=1, device_id=(v, f), device_id_type=MESH)

    for dz in range(1, Z):
        greet(vid(h, zat(dz), x), me_f)
    for dx in range(1, X):
        greet(vid(h, z, xat(dx)), me_f)
    for dx in range(X):
        greet(vid(1 - h, z, xat(dx)), me_f)
    greet(*core_mate)
    greet(*lo_mate)
    greet(*swap_mate)
    acc[...] = jnp.zeros_like(acc)
    pl.semaphore_wait(barrier, (Z - 1) + (X - 1) + X + 3)

    def slot_copy(p, target):
        return pltpu.make_async_remote_copy(
            src_ref=xg.at[p],
            dst_ref=xg.at[p],
            send_sem=ssem.at[0],
            recv_sem=rsem.at[p],
            device_id=target,
            device_id_type=MESH,
        )

    def wait_slot(p):
        slot_copy(p, core_mate).wait_recv()

    swap_copy = pltpu.make_async_remote_copy(
        src_ref=feat_h.at[half_rows],
        dst_ref=xg.at[p0],
        send_sem=ssem.at[1],
        recv_sem=rsem.at[p0],
        device_id=swap_mate,
        device_id_type=MESH,
    )

    @pl.when(h != l)
    def _():
        swap_copy.start()
        swap_copy.wait()

    @pl.when(h == l)
    def _():
        own_copy.wait()

    def forward(p):
        s = l * n_half + p
        count = counts[s]
        block = xg[p]
        zero = jnp.zeros_like(block)
        right = []
        for k in range(SLOTS):
            ok = jnp.logical_and(k < count, cols[k, s] == c)
            r = rows[k, s]
            right.append(
                jnp.concatenate(
                    [
                        jnp.where(jnp.logical_and(ok, r == 0), block, zero),
                        jnp.where(jnp.logical_and(ok, r == 1), block, zero),
                    ],
                    axis=1,
                )
            )
        left = jnp.concatenate([tiles[p * SLOTS + k] for k in range(SLOTS)], axis=1)
        got = dot(left, jnp.concatenate(right, axis=0))
        acc[0] += got[:, :T]
        acc[1] += got[:, T:]

    def pass_z(q, col, p):
        hop = (q + 1) // 2
        sign = sgn(col)

        @pl.when(jnp.logical_and(q % 2 == 1, jnp.logical_or(hop < H - 1, jnp.logical_and(hop == H - 1, sign == 1))))
        def _():
            slot_copy(p, here(zat(1), x)).start()

        @pl.when(jnp.logical_and(q % 2 == 0, jnp.logical_or(hop < H - 1, jnp.logical_and(hop == H - 1, sign == -1))))
        def _():
            slot_copy(p, here(zat(-1), x)).start()

    def begin_z(col, p):
        if H > 1:
            slot_copy(p, here(zat(1), x)).start()
            slot_copy(p, here(zat(-1), x)).start()
        else:
            slot_copy(p, here(zat(1), x)).start()

    @pl.when(c == 0)
    def _():
        for dx in (1, 3, 2):
            slot_copy(p0, here(z, xat(dx))).start()
        begin_z(x, p0)
        tiles_copy.wait()
        forward(p0)

        def from_x(j, carry):
            col = xat(j + 1)
            p = z * X + col
            wait_slot(p)
            begin_z(col, p)
            forward(p)
            return carry

        lax.fori_loop(0, X - 1, from_x, 0)

        def from_z(t, carry):
            q = t // X + 1
            col = xat(t % X)
            p = zat(off(q)) * X + col
            wait_slot(p)
            pass_z(q, col, p)
            forward(p)
            return carry

        lax.fori_loop(0, (Z - 1) * X, from_z, 0)

    @pl.when(c == 1)
    def _():
        begin_z(x, p0)

        def begin_x(p):
            slot_copy(p, here(z, xat(1))).start()
            slot_copy(p, here(z, xat(3))).start()

        begin_x(p0)
        tiles_copy.wait()
        forward(p0)

        def row_x(zz):
            sign = sgn(zz)
            pm = zz * X + xat(-sign)
            pn = zz * X + xat(sign)
            wait_slot(pm)
            slot_copy(pm, here(z, xat(sign))).start()
            forward(pm)
            wait_slot(pn)
            forward(pn)

        def from_z(t, carry):
            q = t + 1
            p = zat(off(q)) * X + x
            wait_slot(p)
            pass_z(q, x, p)
            begin_x(p)
            forward(p)
            row_x(zat(off(q - 1)))
            return carry

        lax.fori_loop(0, Z - 1, from_z, 0)
        row_x(zat(off(Z - 1)))

        def from_far(q, carry):
            p = zat(off(q)) * X + xat(2)
            wait_slot(p)
            forward(p)
            return carry

        lax.fori_loop(0, Z, from_far, 0)

    def exchange(src, dst, i, target):
        return pltpu.make_async_remote_copy(
            src_ref=src,
            dst_ref=dst,
            send_sem=exs.at[i],
            recv_sem=exr.at[i],
            device_id=target,
            device_id_type=MESH,
        )

    first = exchange(acc.at[1 - c], ex.at[0], 0, core_mate)
    first.start()
    first.wait_recv()
    sb[...] = acc[c] + ex[0]
    second = exchange(sb, ex.at[1], 1, lo_mate)
    second.start()
    w_copy.wait()
    bias_copy.wait()
    cot_copy.wait()
    second.wait_recv()
    axf[c] = sb[...] + ex[1]
    third = exchange(axf.at[c], axf.at[c], 2, core_mate)
    third.start()

    def rows_half(r):
        high, low = split(axf[r])
        pre = dot(high, w[...]) + dot(low, w[...]) + bias[...]
        result, slope = gelu_parts(pre)
        where = pl.ds(pl.multiple_of(r * T, T), T)
        out_ref[where, :] = result.astype(BF16)
        grad = (cot[where, :].astype(F32) * slope).astype(BF16)
        gp[r] = grad
        back = dot(w[...], grad, ((1,), (1,)))
        for cc in range(2):
            for ll in range(2):
                pt[cc, r, ll * 32 : ll * 32 + 32, :] = back[ll * 64 + cc * 32 : ll * 64 + cc * 32 + 32, :]

    rows_half(c)
    exchange(axf.at[c], axf.at[1 - c], 2, core_mate).wait_recv()
    rows_half(1 - c)

    p_first = exchange(pt.at[1 - c], pe.at[0], 3, core_mate)
    p_first.start()

    local_w = jnp.zeros((T, T), F32)
    local_b = jnp.zeros((1, T), F32)
    for r in range(2):
        high, low = split(axf[r])
        grad = gp[r]
        local_w += dot(high, grad, ((0,), (0,))) + dot(low, grad, ((0,), (0,)))
        local_b += jnp.sum(grad.astype(F32), axis=0, keepdims=True)
    spread_b = jnp.broadcast_to(local_b, (8, T))
    for i in range(Z):
        gwb[i, :R, :] = local_w[i * R : i * R + R, :]
        gwb[i, R:, :] = spread_b

    def g1_copy(dz):
        return pltpu.make_async_remote_copy(
            src_ref=gwb.at[zat(dz)],
            dst_ref=g1.at[z],
            send_sem=gsem.at[0],
            recv_sem=g1r.at[z],
            device_id=here(zat(dz), x),
            device_id_type=MESH,
        )

    for dz in range(1, Z):
        g1_copy(dz).start()

    p_first.wait_recv()
    pb[...] = pt[c] + pe[0]
    p_second = exchange(pb, pe.at[1], 4, lo_mate)
    p_second.start()
    p_second.wait_recv()
    pf[...] = (pb[...] + pe[1]).astype(BF16)

    def own(p):
        s = l * n_half + p
        count = counts[s]
        low = pf[0]
        high = pf[1]
        zero = jnp.zeros_like(low)
        left = []
        for k in range(SLOTS):
            ok = k < count
            col = cols[k, s]
            picked = jnp.where(rows[k, s] == 0, low, high)
            left.append(
                jnp.concatenate(
                    [
                        jnp.where(jnp.logical_and(ok, col == 0), picked, zero),
                        jnp.where(jnp.logical_and(ok, col == 1), picked, zero),
                    ],
                    axis=0,
                )
            )
        right = tiles[pl.ds(p * SLOTS, SLOTS)].reshape(SLOTS * T, T)
        return dot(jnp.concatenate(left, axis=1), right)

    def sum_copy(i, target):
        return pltpu.make_async_remote_copy(
            src_ref=sbuf.at[i],
            dst_ref=rbuf.at[i],
            send_sem=tsem.at[0],
            recv_sem=trsem.at[i],
            device_id=target,
            device_id_type=MESH,
        )

    def take(i):
        sum_copy(i, core_mate).wait_recv()
        return rbuf[i].astype(F32)

    def put(i, value, target):
        sbuf[i] = value.astype(BF16)
        sum_copy(i, target).start()

    last = Z - 1

    def z_direction(q, col):
        return jnp.where(q == last, sgn(col), 2 * (q % 2) - 1)

    def has_incoming(q, col):
        by_parity = (2 * (q % 2) - 1) == sgn(col)
        return jnp.logical_or(q + 2 < last, jnp.logical_and(q < last, jnp.logical_and(q + 2 >= last, by_parity)))

    def source_q(q):
        return jnp.minimum(q + 2, last)

    def weight_sums_one():
        total = gwb[z]
        for dz in range(1, Z):
            src = zat(dz)
            pltpu.make_async_remote_copy(
                src_ref=gwb.at[src],
                dst_ref=g1.at[src],
                send_sem=gsem.at[0],
                recv_sem=g1r.at[src],
                device_id=here(zat(dz), x),
                device_id_type=MESH,
            ).wait_recv()
            total = total + g1[src]
        g2s[...] = total
        for e in range(1, 2 * X):
            hh = (h + e // X) % 2
            xx = xat(e % X)
            pltpu.make_async_remote_copy(
                src_ref=g2s,
                dst_ref=g2.at[h * X + x],
                send_sem=gsem.at[1],
                recv_sem=g2r.at[h * X + x],
                device_id=(vid(hh, z, xx), me_f),
                device_id_type=MESH,
            ).start()

    def weight_sums_two():
        total = g2s[...]
        for e in range(1, 2 * X):
            hh = (h + e // X) % 2
            xx = xat(e % X)
            src = hh * X + xx
            pltpu.make_async_remote_copy(
                src_ref=g2s,
                dst_ref=g2.at[src],
                send_sem=gsem.at[1],
                recv_sem=g2r.at[src],
                device_id=(vid(hh, z, xx), me_f),
                device_id_type=MESH,
            ).wait_recv()
            total = total + g2[src]
        g3[z] = total[:R, :]
        gb_ref[...] = total[R : R + 1, :]
        for dz in range(1, Z):
            pltpu.make_async_remote_copy(
                src_ref=g3.at[z],
                dst_ref=g3.at[z],
                send_sem=gsem.at[2],
                recv_sem=g3r.at[z],
                device_id=here(zat(dz), x),
                device_id_type=MESH,
            ).start()

    def finish(total):
        for lp in range(2):
            for ct in range(2):
                fs[lp, ct] = total[ct * 64 + lp * 32 : ct * 64 + lp * 32 + 32, :]

    ZB = Z * X - X

    @pl.when(c == 0)
    def _():
        def along_z(t, carry):
            q = last - t // X
            col = xat(t % X + 1)
            value = own(((z + Z - off(q)) % Z) * X + col)
            i = (q - 1) * X + col
            d = z_direction(q, col)
            target = here((z + Z + d) % Z, x)

            @pl.when(has_incoming(q, col))
            def _():
                put(i, value + take((source_q(q) - 1) * X + col), target)

            @pl.when(jnp.logical_not(has_incoming(q, col)))
            def _():
                put(i, value, target)

            return carry

        half = (Z - 1) * X // 2
        lax.fori_loop(0, half, along_z, 0)
        weight_sums_one()
        lax.fori_loop(half, (Z - 1) * X, along_z, 0)

        def total_of(col):
            value = own(z * X + col) + take(col)
            if Z > 2:
                value = value + take(X + col)
            return value

        def to_x(j, carry):
            col = xat(j)
            sbuf_i = ZB + x
            value = total_of(col)
            sbuf[ZB + X + j] = value.astype(BF16)
            pltpu.make_async_remote_copy(
                src_ref=sbuf.at[ZB + X + j],
                dst_ref=rbuf.at[sbuf_i],
                send_sem=tsem.at[0],
                recv_sem=trsem.at[sbuf_i],
                device_id=here(z, col),
                device_id_type=MESH,
            ).start()
            return carry

        lax.fori_loop(1, X, to_x, 0)
        total = total_of(x)
        weight_sums_two()
        for dx in range(1, X):
            total = total + take(ZB + xat(dx))
        finish(total)

    @pl.when(c == 1)
    def _():
        def opposite(t, carry):
            q = last - t
            zz = (z + Z - off(q)) % Z
            put(zz, own(zz * X + xat(2)), here(z, xat(sgn(zz))))
            return carry

        lax.fori_loop(0, Z, opposite, 0)

        def beside(t, carry):
            q = last - t
            zz = (z + Z - off(q)) % Z
            sign = sgn(zz)
            against = own(zz * X + xat(-sign))
            put(2 * Z + zz, against, here(z, xat(-sign)))
            along = own(zz * X + xat(sign)) + take(zz)
            put(Z + zz, along, here(z, xat(sign)))
            return carry

        lax.fori_loop(0, Z, beside, 0)
        weight_sums_one()

        def row_total(zz):
            return own(zz * X + x) + take(Z + zz) + take(2 * Z + zz)

        def along_z(t, carry):
            q = last - t
            value = row_total((z + Z - off(q)) % Z)
            i = 3 * Z + q
            d = z_direction(q, x)
            target = here((z + Z + d) % Z, x)

            @pl.when(has_incoming(q, x))
            def _():
                put(i, value + take(3 * Z + source_q(q)), target)

            @pl.when(jnp.logical_not(has_incoming(q, x)))
            def _():
                put(i, value, target)

            return carry

        lax.fori_loop(0, Z - 1, along_z, 0)
        total = row_total(z)
        weight_sums_two()
        total = total + take(3 * Z + 1)
        if Z > 2:
            total = total + take(3 * Z + 2)
        finish(total)

    def final_copy(lp, slot, target):
        return pltpu.make_async_remote_copy(
            src_ref=fs.at[lp],
            dst_ref=fr.at[slot],
            send_sem=fsem.at[lp],
            recv_sem=frsem.at[slot],
            device_id=target,
            device_id_type=MESH,
        )

    for lp in range(2):
        is_self = jnp.logical_and(h == l, l == lp)

        @pl.when(jnp.logical_not(is_self))
        def _():
            final_copy(lp, h, (vid(l, z, x), lp * 2 + c)).start()

        @pl.when(is_self)
        def _():
            fr[h] = fs[lp]

    for dz in range(1, Z):
        src = zat(dz)
        pltpu.make_async_remote_copy(
            src_ref=g3.at[src],
            dst_ref=g3.at[src],
            send_sem=gsem.at[2],
            recv_sem=g3r.at[src],
            device_id=here(zat(dz), x),
            device_id_type=MESH,
        ).wait_recv()
    gw_ref[...] = g3[...].reshape(T, T)

    for hs in range(2):

        @pl.when(jnp.logical_not(jnp.logical_and(h == l, h == hs)))
        def _():
            final_copy(0, hs, lo_mate).wait_recv()

    both = fr[0] + fr[1]
    for ct in range(2):
        gf_ref[:, ct * T : ct * T + T] = both[ct].astype(BF16)

    for lp in range(2):

        @pl.when(jnp.logical_not(jnp.logical_and(h == l, l == lp)))
        def _():
            final_copy(lp, h, (vid(l, z, x), lp * 2 + c)).wait_send()

    first.wait_send()
    second.wait_send()
    third.wait_send()
    p_first.wait_send()
    p_second.wait_send()
    n_sent = Z * X - 1

    def drained(ref, sem):
        pltpu.make_async_remote_copy(
            src_ref=ref,
            dst_ref=ref,
            send_sem=sem,
            recv_sem=rsem.at[0],
            device_id=core_mate,
            device_id_type=MESH,
        ).wait_send()

    drained(xg.at[pl.ds(0, n_sent)], ssem.at[0])
    drained(rbuf.at[pl.ds(0, n_sent)], tsem.at[0])
    drained(g1.at[pl.ds(0, Z - 1)], gsem.at[0])
    drained(g2.at[pl.ds(0, 2 * X - 1)], gsem.at[1])
    drained(g3.at[pl.ds(0, Z - 1)], gsem.at[2])


def on_device(features, weight, bias, cotangent, adj_tiles, tile_rows, tile_cols, tile_counts):
    X = RING_X
    Z = lax.axis_size("vtx") // (2 * X)
    n_half = Z * X
    R = T // Z
    anywhere = pl.BlockSpec(memory_space=pl.ANY)
    smem = pl.BlockSpec(memory_space=pltpu.SMEM)
    vmem = pl.BlockSpec(memory_space=pltpu.VMEM)
    n_buf = 4 * Z + 2 * X
    out, gf, gw, gb = pl.pallas_call(
        functools.partial(kernel, Z),
        out_shape=(
            jax.ShapeDtypeStruct((2 * T, T), BF16),
            jax.ShapeDtypeStruct((32, 2 * T), BF16),
            jax.ShapeDtypeStruct((T, T), F32),
            jax.ShapeDtypeStruct((1, T), F32),
        ),
        in_specs=[anywhere] * 5 + [smem] * 3,
        out_specs=(vmem, vmem, vmem, vmem),
        scratch_shapes=[
            pltpu.VMEM((n_half, T, T), BF16),
            pltpu.VMEM((n_half * SLOTS, T, T), BF16),
            pltpu.VMEM((T, T), BF16),
            pltpu.VMEM((1, T), F32),
            pltpu.VMEM((2 * T, T), BF16),
            pltpu.VMEM((2, T, T), F32),
            pltpu.VMEM((2, T, T), F32),
            pltpu.VMEM((T, T), F32),
            pltpu.VMEM((2, T, T), F32),
            pltpu.VMEM((2, T, T), BF16),
            pltpu.VMEM((2, 2, 64, T), F32),
            pltpu.VMEM((2, 2, 64, T), F32),
            pltpu.VMEM((2, 64, T), F32),
            pltpu.VMEM((2, 64, T), BF16),
            pltpu.VMEM((Z, R + 8, T), F32),
            pltpu.VMEM((Z, R + 8, T), F32),
            pltpu.VMEM((R + 8, T), F32),
            pltpu.VMEM((2 * X, R + 8, T), F32),
            pltpu.VMEM((Z, R, T), F32),
            pltpu.VMEM((n_buf, T, T), BF16),
            pltpu.VMEM((n_buf, T, T), BF16),
            pltpu.VMEM((2, 2, 32, T), F32),
            pltpu.VMEM((2, 2, 32, T), F32),
            pltpu.SemaphoreType.DMA((5,)),
            pltpu.SemaphoreType.DMA((2,)),
            pltpu.SemaphoreType.DMA((n_half,)),
            pltpu.SemaphoreType.DMA((5,)),
            pltpu.SemaphoreType.DMA((5,)),
            pltpu.SemaphoreType.DMA((3,)),
            pltpu.SemaphoreType.DMA((Z,)),
            pltpu.SemaphoreType.DMA((2 * X,)),
            pltpu.SemaphoreType.DMA((Z,)),
            pltpu.SemaphoreType.DMA((1,)),
            pltpu.SemaphoreType.DMA((n_buf,)),
            pltpu.SemaphoreType.DMA((2,)),
            pltpu.SemaphoreType.DMA((2,)),
        ],
        compiler_params=pltpu.CompilerParams(
            collective_id=0, has_side_effects=True, vmem_limit_bytes=60 * 1024 * 1024
        ),
        cost_estimate=pl.CostEstimate(flops=2 * 10**9, bytes_accessed=5 * 10**6, transcendentals=32768),
    )(features, weight, bias.reshape(1, T), cotangent, adj_tiles, tile_rows.T, tile_cols.T, tile_counts)
    return out, gf.T, gw, gb.reshape(T)


def solution(mesh):
    in_specs = (
        P("vtx", None),
        P(None, "feat"),
        P("feat"),
        P("vtx", "feat"),
        P("vtx", None, None),
        P("vtx", None),
        P("vtx", None),
        P("vtx"),
    )
    out_specs = (P("vtx", "feat"), P("vtx", "feat"), P(None, "feat"), P("feat"))
    return jax.shard_map(on_device, mesh=mesh, in_specs=in_specs, out_specs=out_specs, check_vma=False)
```

time: 2090 us -> 71.9 us (0.03)
  waiting for transfers between devices: 733 us -> 0 us
  starting transfers between devices: 506 us -> 0 us
  local copies, waits for them, and re-layouts: 293 us -> 5.43 us
  matrix products: 252 us -> 0 us
  blocking collectives: 186 us -> 0 us
  other arithmetic: 87.9 us -> 0 us
  Pallas kernels: 0 us -> 65.5 us
    ppermute x63 -> x0, starting transfers between devices: 506 us -> none  [passed_along(): return lax.ppermute(value, axis, pairs)]
    psum x1 -> x0, waiting for transfers between devices: 418 us -> none  [on_device(): grad_weight, grad_bias = lax.psum((local_weight, local_bias), 'vtx')]
    dot_general x259 -> x0, matrix products: 252 us -> none  [the longest x128 101 us: tile_products(): jnp.einsum('kr,kic->ric', onehot, prod, precision=lax.Precision.HIGHEST)]
    dynamic_slice x193 -> x0, local copies, waits for them, and re-layouts: 214 us -> none  [the longest x64 79.6 us: own_term(): tile_counts[target]]
    psum x1 -> x0, blocking collectives: 186 us -> none  [on_device(): grad_weight, grad_bias = lax.psum((local_weight, local_bias), 'vtx')]
    ppermute x63 -> x0, waiting for transfers between devices: 168 us -> none  [passed_along(): return lax.ppermute(value, axis, pairs)]
    all_gather x1 -> x0, waiting for transfers between devices: 129 us -> none  [on_device(): piece = lax.all_gather(hidden, 'vtx', axis=0, tiled=True)]
    convert_element_type x129 -> x0, other arithmetic: 84.2 us -> none  [the longest x128 82.8 us: tile_products(): (jnp.arange(tiles_here.shape[0], dtype=jnp.int32) < count).astype(jnp.flo...]
  transfers between devices with their start and end apart: 66 -> 0, of which waited for: 66 -> 0; matrix products, arithmetic and copies ran while one was open for 0% -> 0% of each run, Pallas kernels for 0% -> 0%
where the time goes in v1:
time: 71.9 us; the launch traced here: 71.6 us
  Pallas kernels  65.5 us (91%)
  local copies, waits for them, and re-layouts  5.43 us (8%)
    pallas_call x1, Pallas kernels, on_device(): pl.pallas_call(functools.partial(kernel, Z), out_shape=(jax.ShapeDtypeStr...  65.5 us
    unnamed x4, local copies, waits for them, and re-layouts  5.43 us

profile of v1, /device:TPU:2, one launch (start us, length us, event | category | flops | bytes accessed | tf_op | source)
XLA Modules:
  0.0 71.6 jit_solution(12409351474729731164)
XLA Ops:
  0.6 65.5 %shard_map.111 = (bf16[256,128]{1,0:T(8,128)(2,1)}, bf16[32,256]{1,0:T(8,128)(2,1)}, f32[128,128]{1,0:T(8,128)}, f32[1,128]{1,0:T(1,128)}) custom-call(bf16[256,128]{1,0:T(8,128)(2,1)} %feat_h.1, bf16[128,128]{1,0:T(8,128)(2,1)} %weight_h.1, f32[1,128]{1,0:T(1,128)} %bitcast.8, bf16[256,128]{1,0:T(8,128)(2,1)} %cot_h.1, bf16[256,128,128]{2,1,0:T(8,128)(2,1)} %tiles_h.1, ...), custom_call_target="tpu_custom_call" | custom-call | flops 2000000000 | bytes 5000000 | tf_op jit(solution)/shard_map/pallas_call | solution.py:678
  66.2 1.5 %copy.16 = bf16[256,128]{1,0:T(8,128)(2,1)} copy(bf16[256,128]{1,0:T(8,128)(2,1)} %get-tuple-element.16) | data formatting | bytes 131072
  67.7 1.3 %copy.17 = bf16[256,32]{0,1:T(8,128)(2,1)} copy(bf16[256,32]{0,1:T(8,128)(2,1)} %bitcast.5) | data formatting | bytes 32768
  69.0 1.5 %copy.18 = f32[128,128]{1,0:T(8,128)} copy(f32[128,128]{1,0:T(8,128)} %get-tuple-element.18) | data formatting | bytes 131072
  70.5 1.2 %copy.19 = f32[128]{0:T(128)} copy(f32[128]{0:T(128)} %bitcast.9) | data formatting | bytes 1024

commit v2 on v1

v2 whole, which is shorter than its diff:
```python
import functools
import math

import jax
import jax.numpy as jnp
from jax import lax
from jax.experimental import pallas as pl
from jax.experimental.pallas import tpu as pltpu
from jax.sharding import PartitionSpec as P

MESH = pl.DeviceIdType.MESH
RING_X = 4
T = 128
SLOTS = 4
F32 = jnp.float32
BF16 = jnp.bfloat16


def dot(a, b, dims=((1,), (0,))):
    return lax.dot_general(a, b, (dims, ((), ())), preferred_element_type=F32)


def split(v):
    high = v.astype(BF16)
    return high, (v - high.astype(F32)).astype(BF16)


def gelu_parts(v):
    c = math.sqrt(2.0 / math.pi)
    t = jnp.tanh(c * (v + 0.044715 * (v * v * v)))
    cdf = 0.5 * (1.0 + t)
    slope = cdf + 0.5 * v * (1.0 - t * t) * (c * (1.0 + (3.0 * 0.044715) * (v * v)))
    return v * cdf, slope


def kernel(
    Z,
    feat_h,
    weight_h,
    bias_h,
    cot_h,
    tiles_h,
    rows_h,
    cols_h,
    counts_h,
    out_ref,
    gf_ref,
    gw_ref,
    gb_ref,
    rows,
    cols,
    counts,
    mine,
    xg,
    tiles,
    w,
    bias,
    cot,
    acc,
    ex,
    sb,
    axf,
    gp,
    pt,
    pe,
    pb,
    pf,
    gwb,
    g1,
    g2s,
    g2,
    g3,
    sbuf,
    rbuf,
    fs,
    fr,
    lsem,
    ssem,
    rsem,
    exs,
    exr,
    gsem,
    g1r,
    g2r,
    g3r,
    tsem,
    trsem,
    fsem,
    frsem,
):
    X = RING_X
    E = 2 * X
    R = T // E
    NEAR = 3
    me_v = lax.axis_index("vtx")
    me_f = lax.axis_index("feat")
    h = me_v // (Z * X)
    z = (me_v // X) % Z
    x = me_v % X
    l = me_f // 2
    c = me_f % 2

    def vid(hh, zz, xx):
        return (hh * Z + zz) * X + xx

    def here(zz, xx):
        return (vid(h, zz, xx), me_f)

    core_mate = (me_v, l * 2 + 1 - c)
    lo_mate = (me_v, (1 - l) * 2 + c)

    def zat(o):
        return (z + 2 * Z + o) % Z

    def xat(o):
        return (x + X + o) % X

    def offset(q):
        return ((q + 1) // 2) * (1 - 2 * (q % 2))

    p0 = z * X + x

    half_rows = pl.ds(pl.multiple_of(c * T, T), T)
    n_half = Z * X
    tiles_copy = pltpu.make_async_copy(
        tiles_h.at[pl.ds(l * (n_half * SLOTS), n_half * SLOTS)], tiles, lsem.at[0]
    )
    w_copy = pltpu.make_async_copy(weight_h, w, lsem.at[1])
    bias_copy = pltpu.make_async_copy(bias_h, bias, lsem.at[2])
    cot_copy = pltpu.make_async_copy(cot_h, cot, lsem.at[3])
    own_copy = pltpu.make_async_copy(feat_h.at[half_rows], mine, lsem.at[4])

    index_copies = [
        pltpu.make_async_copy(src, dst, lsem.at[5 + i])
        for i, (src, dst) in enumerate(((rows_h, rows), (cols_h, cols), (counts_h, counts)))
    ]
    own_copy.start()
    for copy in index_copies:
        copy.start()
    tiles_copy.start()
    w_copy.start()
    bias_copy.start()
    cot_copy.start()

    barrier = pltpu.get_barrier_semaphore()

    def greet(v, f):
        pl.semaphore_signal(barrier, inc=1, device_id=(v, f), device_id_type=MESH)

    for q in reversed(range(1, Z)):
        zz = zat(offset(q))
        greet(vid(1 - h, zz, x), h * 2 + c)
        greet(vid(h, zz, x), h * 2 + c)

        @pl.when(h != l)
        def _():
            greet(vid(h, zz, x), me_f)

    for dx in (2, 1, 3):

        @pl.when(h != l)
        def _():
            greet(vid(1 - h, z, xat(dx)), h * 2 + c)
            greet(vid(h, z, xat(dx)), h * 2 + c)

        greet(vid(1 - h, z, xat(dx)), me_f)
        greet(vid(h, z, xat(dx)), me_f)
    greet(vid(1 - h, z, x), h * 2 + c)
    greet(*lo_mate)
    greet(*core_mate)

    @pl.when(h != l)
    def _():
        greet(vid(1 - h, z, x), me_f)

    acc[...] = jnp.zeros_like(acc)
    own_copy.wait()

    @pl.when(h == l)
    def _():
        xg[p0] = mine[...]

    n_greet = 2 * (Z - 1) + 3 * (X - 1) + 3

    @pl.when(h == l)
    def _():
        pl.semaphore_wait(barrier, n_greet)

    @pl.when(h != l)
    def _():
        pl.semaphore_wait(barrier, n_greet + Z)


    def slot_copy(p, target):
        return pltpu.make_async_remote_copy(
            src_ref=xg.at[p],
            dst_ref=xg.at[p],
            send_sem=ssem.at[0],
            recv_sem=rsem.at[p],
            device_id=target,
            device_id_type=MESH,
        )

    def wait_slot(p):
        slot_copy(p, core_mate).wait_recv()

    def first_copy(zz, xx):
        return pltpu.make_async_remote_copy(
            src_ref=mine,
            dst_ref=xg.at[p0],
            send_sem=ssem.at[0],
            recv_sem=rsem.at[p0],
            device_id=(vid(l, zz, xx), h * 2 + c),
            device_id_type=MESH,
        )

    for dx in (2, 1, 3):
        first_copy(z, xat(dx)).start()
    first_copy(zat(offset(3)), x).start()
    first_copy(zat(offset(4)), x).start()
    first_copy(zat(offset(5)), x).start()
    first_copy(zat(offset(6)), x).start()

    @pl.when(h != l)
    def _():
        first_copy(z, x).start()

    def forward(p):
        s = l * n_half + p
        count = counts[s]
        block = xg[p]
        zero = jnp.zeros_like(block)
        right = []
        for k in range(SLOTS):
            ok = jnp.logical_and(k < count, cols[k, s] == c)
            r = rows[k, s]
            right.append(
                jnp.concatenate(
                    [
                        jnp.where(jnp.logical_and(ok, r == 0), block, zero),
                        jnp.where(jnp.logical_and(ok, r == 1), block, zero),
                    ],
                    axis=1,
                )
            )
        left = jnp.concatenate([tiles[p * SLOTS + k] for k in range(SLOTS)], axis=1)
        got = dot(left, jnp.concatenate(right, axis=0))
        acc[0] += got[:, :T]
        acc[1] += got[:, T:]

    def far_row(q):
        p = zat(offset(q)) * X + x
        wait_slot(p)
        for dx in (2, 1, 3):
            slot_copy(p, here(z, xat(dx))).start()

    def arrived(q, dx):
        p = zat(offset(q)) * X + xat(dx)
        wait_slot(p)
        forward(p)

    far_row(3)
    far_row(4)
    first_copy(zat(offset(7)), x).start()
    for copy in index_copies:
        copy.wait()
    tiles_copy.wait()

    @pl.when(h != l)
    def _():
        wait_slot(p0)

    forward(p0)
    far_row(5)
    far_row(6)
    first_copy(zat(offset(1)), x).start()
    first_copy(zat(offset(2)), x).start()
    for dx in (1, 3, 2):
        p = z * X + xat(dx)
        wait_slot(p)
        slot_copy(p, here(zat(1), x)).start()
        slot_copy(p, here(zat(-1), x)).start()
    forward(zat(offset(3)) * X + x)
    forward(zat(offset(4)) * X + x)
    far_row(7)
    forward(zat(offset(5)) * X + x)
    forward(zat(offset(6)) * X + x)
    forward(zat(offset(7)) * X + x)

    def this_row(dx, carry):
        forward(z * X + xat(dx))
        return carry

    lax.fori_loop(1, X, this_row, 0)
    arrived(1, 0)
    arrived(2, 0)

    def beside(t, carry):
        arrived(t // 3 + 1, t % 3 + 1)
        return carry

    lax.fori_loop(0, 6, beside, 0)

    def far(t, carry):
        arrived(NEAR + t // 3, t % 3 + 1)
        return carry

    lax.fori_loop(0, (Z - NEAR) * 3, far, 0)

    def exchange(src, dst, i, target):
        return pltpu.make_async_remote_copy(
            src_ref=src,
            dst_ref=dst,
            send_sem=exs.at[i],
            recv_sem=exr.at[i],
            device_id=target,
            device_id_type=MESH,
        )

    first = exchange(acc.at[1 - c], ex.at[0], 0, core_mate)
    first.start()
    first.wait_recv()
    sb[...] = acc[c] + ex[0]
    second = exchange(sb, ex.at[1], 1, lo_mate)
    second.start()
    w_copy.wait()
    bias_copy.wait()
    cot_copy.wait()
    second.wait_recv()
    axf[c] = sb[...] + ex[1]
    third = exchange(axf.at[c], axf.at[c], 2, core_mate)
    third.start()

    def rows_half(r):
        high, low = split(axf[r])
        pre = dot(high, w[...]) + dot(low, w[...]) + bias[...]
        result, slope = gelu_parts(pre)
        where = pl.ds(pl.multiple_of(r * T, T), T)
        out_ref[where, :] = result.astype(BF16)
        grad = (cot[where, :].astype(F32) * slope).astype(BF16)
        gp[r] = grad
        back = dot(w[...], grad, ((1,), (1,)))
        for cc in range(2):
            for ll in range(2):
                pt[cc, r, ll * 32 : ll * 32 + 32, :] = back[ll * 64 + cc * 32 : ll * 64 + cc * 32 + 32, :]

    rows_half(c)
    exchange(axf.at[c], axf.at[1 - c], 2, core_mate).wait_recv()
    rows_half(1 - c)

    p_first = exchange(pt.at[1 - c], pe.at[0], 3, core_mate)
    p_first.start()

    local_w = jnp.zeros((T, T), F32)
    local_b = jnp.zeros((1, T), F32)
    for r in range(2):
        high, low = split(axf[r])
        grad = gp[r]
        local_w += dot(high, grad, ((0,), (0,))) + dot(low, grad, ((0,), (0,)))
        local_b += jnp.sum(grad.astype(F32), axis=0, keepdims=True)
    spread_b = jnp.broadcast_to(local_b, (8, T))
    for i in range(E):
        gwb[i, :R, :] = local_w[i * R : i * R + R, :]
        gwb[i, R:, :] = spread_b

    me_e = h * X + x

    def e_at(i):
        hh = (h + i // X) % 2
        xx = xat(i % X)
        return hh * X + xx, (vid(hh, z, xx), me_f)

    def weight_copy(src, dst, send, recv, target):
        return pltpu.make_async_remote_copy(
            src_ref=src, dst_ref=dst, send_sem=send, recv_sem=recv, device_id=target, device_id_type=MESH
        )

    for i in range(1, E):
        e, target = e_at(i)
        weight_copy(gwb.at[e], g1.at[me_e], gsem.at[0], g1r.at[me_e], target).start()

    p_first.wait_recv()
    pb[...] = pt[c] + pe[0]
    p_second = exchange(pb, pe.at[1], 4, lo_mate)
    p_second.start()
    p_second.wait_recv()
    pf[...] = (pb[...] + pe[1]).astype(BF16)

    def own(p):
        s = l * n_half + p
        count = counts[s]
        low = pf[0]
        high = pf[1]
        zero = jnp.zeros_like(low)
        left = []
        for k in range(SLOTS):
            ok = k < count
            col = cols[k, s]
            picked = jnp.where(rows[k, s] == 0, low, high)
            left.append(
                jnp.concatenate(
                    [
                        jnp.where(jnp.logical_and(ok, col == 0), picked, zero),
                        jnp.where(jnp.logical_and(ok, col == 1), picked, zero),
                    ],
                    axis=0,
                )
            )
        right = tiles[pl.ds(p * SLOTS, SLOTS)].reshape(SLOTS * T, T)
        return dot(jnp.concatenate(left, axis=1), right)

    def sum_copy(i, target):
        return pltpu.make_async_remote_copy(
            src_ref=sbuf.at[i],
            dst_ref=rbuf.at[i],
            send_sem=tsem.at[0],
            recv_sem=trsem.at[i],
            device_id=target,
            device_id_type=MESH,
        )

    def take(i):
        sum_copy(i, core_mate).wait_recv()
        return rbuf[i].astype(F32)

    def put(i, value, target):
        sbuf[i] = value.astype(BF16)
        sum_copy(i, target).start()

    def weight_sums_one():
        total = gwb[me_e]
        for i in range(1, E):
            e, target = e_at(i)
            weight_copy(gwb.at[e], g1.at[e], gsem.at[0], g1r.at[e], target).wait_recv()
            total = total + g1[e]
        g2s[...] = total
        for dz in range(1, Z):
            weight_copy(g2s, g2.at[z], gsem.at[1], g2r.at[z], here(zat(dz), x)).start()

    def weight_sums_two():
        total = g2s[...]
        for dz in range(1, Z):
            zz = zat(dz)
            weight_copy(g2s, g2.at[zz], gsem.at[1], g2r.at[zz], here(zz, x)).wait_recv()
            total = total + g2[zz]
        g3[me_e] = total[:R, :]
        gb_ref[...] = total[R : R + 1, :]
        for i in range(1, E):
            e, target = e_at(i)
            weight_copy(g3.at[me_e], g3.at[me_e], gsem.at[2], g3r.at[me_e], target).start()

    def row_to(q):
        return zat(-offset(q))

    NS = Z + X - 1

    def final_copy(i, lp, slot, target):
        return pltpu.make_async_remote_copy(
            src_ref=fs.at[i, lp],
            dst_ref=fr.at[slot],
            send_sem=fsem.at[0],
            recv_sem=frsem.at[slot],
            device_id=target,
            device_id_type=MESH,
        )

    def deliver(value, i, zz, xx):
        value = value.astype(BF16)
        for lp in range(2):
            for ct in range(2):
                fs[i, lp, ct] = value[ct * 64 + lp * 32 : ct * 64 + lp * 32 + 32, :]
            is_self = jnp.logical_and(jnp.logical_and(h == l, l == lp), i == 0)

            @pl.when(jnp.logical_not(is_self))
            def _():
                final_copy(i, lp, h * NS + i, (vid(l, zz, xx), lp * 2 + c)).start()

            @pl.when(is_self)
            def _():
                fr[h * NS + i] = fs[i, lp]

    def far_x(t, carry):
        zz = row_to(Z - 1 - t)
        for dx in (2, 1, 3):
            put(zz * 3 + dx - 1, own(zz * X + xat(dx)), here(z, xat(dx)))
        return carry

    def beside_z(t, carry):
        q, dx = t // 3 + 1, t % 3 + 1
        zz = row_to(q)
        put(3 * Z + t, own(zz * X + xat(dx)), here(zz, x))
        return carry

    def both_ways(t, carry):
        far_x(t, carry)
        return beside_z(t, carry)

    first_part = min(Z - NEAR, 6)
    lax.fori_loop(0, first_part, both_ways, 0)
    lax.fori_loop(first_part, Z - NEAR, far_x, 0)
    lax.fori_loop(first_part, 6, beside_z, 0)

    def same_column(q, carry):
        zz = row_to(q)
        deliver(own(zz * X + x), q, zz, x)
        return carry

    lax.fori_loop(0, NEAR, same_column, 0)
    weight_sums_one()

    def this_row_x(dx, carry):
        value = own(z * X + xat(dx)) + take(3 * Z + dx - 1) + take(3 * Z + 3 + dx - 1)
        deliver(value, Z - 1 + dx, z, xat(dx))
        return carry

    lax.fori_loop(1, X, this_row_x, 0)

    def far_z(t, carry):
        q = Z - 1 - t
        zz = row_to(q)
        value = own(zz * X + x)
        for dx in (1, 3, 2):
            value = value + take(zz * 3 + dx - 1)
        deliver(value, q, zz, x)
        return carry

    lax.fori_loop(0, Z - NEAR, far_z, 0)
    weight_sums_two()

    def collect(slot, total):
        is_self = jnp.logical_and(h == l, slot == h * NS)

        @pl.when(jnp.logical_not(is_self))
        def _():
            final_copy(0, 0, slot, core_mate).wait_recv()

        return total + fr[slot].astype(F32)

    both = lax.fori_loop(0, 2 * NS, collect, jnp.zeros((2, 32, T), F32))
    for ct in range(2):
        gf_ref[:, ct * T : ct * T + T] = both[ct].astype(BF16)

    for i in range(1, E):
        e, target = e_at(i)
        weight_copy(g3.at[e], g3.at[e], gsem.at[2], g3r.at[e], target).wait_recv()
    gw_ref[...] = g3[...].reshape(T, T)

    first.wait_send()
    second.wait_send()
    third.wait_send()
    p_first.wait_send()
    p_second.wait_send()
    n_sent = Z * X - 1

    def drained(ref, sem):
        pltpu.make_async_remote_copy(
            src_ref=ref,
            dst_ref=ref,
            send_sem=sem,
            recv_sem=rsem.at[0],
            device_id=core_mate,
            device_id_type=MESH,
        ).wait_send()

    drained(xg.at[pl.ds(0, n_sent)], ssem.at[0])
    drained(rbuf.at[pl.ds(0, 3 * (Z - NEAR) + 6)], tsem.at[0])
    drained(fr.at[pl.ds(0, 2 * NS - 1)], fsem.at[0])

    @pl.when(h != l)
    def _():
        drained(mine, ssem.at[0])
        drained(fr.at[0], fsem.at[0])

    drained(g1.at[pl.ds(0, E - 1)], gsem.at[0])
    drained(g2.at[pl.ds(0, Z - 1)], gsem.at[1])
    drained(g3.at[pl.ds(0, E - 1)], gsem.at[2])


def write_out(*refs):
    for source, target in zip(refs[:4], refs[4:]):
        target[...] = source[...]


def on_device(features, weight, bias, cotangent, adj_tiles, tile_rows, tile_cols, tile_counts):
    X = RING_X
    Z = lax.axis_size("vtx") // (2 * X)
    n_half = Z * X
    E = 2 * X
    R = T // E
    n_final = Z + X - 1
    anywhere = pl.BlockSpec(memory_space=pl.ANY)
    vmem = pl.BlockSpec(memory_space=pltpu.VMEM)
    n_buf = 3 * Z + 6
    out, gf, gw, gb = pl.pallas_call(
        functools.partial(kernel, Z),
        out_shape=(
            jax.ShapeDtypeStruct((2 * T, T), BF16),
            jax.ShapeDtypeStruct((32, 2 * T), BF16),
            jax.ShapeDtypeStruct((T, T), F32),
            jax.ShapeDtypeStruct((1, T), F32),
        ),
        in_specs=[anywhere] * 8,
        out_specs=(vmem, vmem, vmem, vmem),
        scratch_shapes=[
            pltpu.SMEM((SLOTS, 2 * n_half), jnp.int32),
            pltpu.SMEM((SLOTS, 2 * n_half), jnp.int32),
            pltpu.SMEM((2 * n_half,), jnp.int32),
            pltpu.VMEM((T, T), BF16),
            pltpu.VMEM((n_half, T, T), BF16),
            pltpu.VMEM((n_half * SLOTS, T, T), BF16),
            pltpu.VMEM((T, T), BF16),
            pltpu.VMEM((1, T), F32),
            pltpu.VMEM((2 * T, T), BF16),
            pltpu.VMEM((2, T, T), F32),
            pltpu.VMEM((2, T, T), F32),
            pltpu.VMEM((T, T), F32),
            pltpu.VMEM((2, T, T), F32),
            pltpu.VMEM((2, T, T), BF16),
            pltpu.VMEM((2, 2, 64, T), F32),
            pltpu.VMEM((2, 2, 64, T), F32),
            pltpu.VMEM((2, 64, T), F32),
            pltpu.VMEM((2, 64, T), BF16),
            pltpu.VMEM((E, R + 8, T), F32),
            pltpu.VMEM((E, R + 8, T), F32),
            pltpu.VMEM((R + 8, T), F32),
            pltpu.VMEM((Z, R + 8, T), F32),
            pltpu.VMEM((E, R, T), F32),
            pltpu.VMEM((n_buf, T, T), BF16),
            pltpu.VMEM((n_buf, T, T), BF16),
            pltpu.VMEM((n_final, 2, 2, 32, T), BF16),
            pltpu.VMEM((2 * n_final, 2, 32, T), BF16),
            pltpu.SemaphoreType.DMA((8,)),
            pltpu.SemaphoreType.DMA((1,)),
            pltpu.SemaphoreType.DMA((n_half,)),
            pltpu.SemaphoreType.DMA((5,)),
            pltpu.SemaphoreType.DMA((5,)),
            pltpu.SemaphoreType.DMA((3,)),
            pltpu.SemaphoreType.DMA((E,)),
            pltpu.SemaphoreType.DMA((Z,)),
            pltpu.SemaphoreType.DMA((E,)),
            pltpu.SemaphoreType.DMA((1,)),
            pltpu.SemaphoreType.DMA((n_buf,)),
            pltpu.SemaphoreType.DMA((1,)),
            pltpu.SemaphoreType.DMA((2 * n_final,)),
        ],
        compiler_params=pltpu.CompilerParams(
            collective_id=0, has_side_effects=True, vmem_limit_bytes=60 * 1024 * 1024
        ),
        cost_estimate=pl.CostEstimate(flops=2 * 10**9, bytes_accessed=5 * 10**6, transcendentals=32768),
    )(features, weight, bias.reshape(1, T), cotangent, adj_tiles, tile_rows.T, tile_cols.T, tile_counts)
    results = (out, gf, gw, gb)
    out, gf, gw, gb = pl.pallas_call(
        write_out,
        out_shape=tuple(jax.ShapeDtypeStruct(a.shape, a.dtype) for a in results),
        in_specs=[vmem] * 4,
        out_specs=(vmem,) * 4,
    )(*results)
    return out, gf.T, gw, gb.reshape(T)


def solution(mesh):
    in_specs = (
        P("vtx", None),
        P(None, "feat"),
        P("feat"),
        P("vtx", "feat"),
        P("vtx", None, None),
        P("vtx", None),
        P("vtx", None),
        P("vtx"),
    )
    out_specs = (P("vtx", "feat"), P("vtx", "feat"), P(None, "feat"), P("feat"))
    return jax.shard_map(on_device, mesh=mesh, in_specs=in_specs, out_specs=out_specs, check_vma=False)
```

time: 71.9 us -> 62.4 us (0.87)
  the two profiles are of different devices: /device:TPU:2 before, /device:TPU:32 now
where the time goes in v2:
time: 62.4 us; the launch traced here: 62.3 us
  Pallas kernels  61.6 us (99%)
  between operations  0.64 us (1%)
    pallas_call x1, Pallas kernels, on_device(): pl.pallas_call(functools.partial(kernel, Z), out_shape=(jax.ShapeDtypeStr...  60.1 us
    pallas_call x1, Pallas kernels, on_device(): pl.pallas_call(write_out, out_shape=tuple((jax.ShapeDtypeStruct(a.shape,...  1.55 us

profile of v2, /device:TPU:32, one launch (start us, length us, event | category | flops | bytes accessed | tf_op | source)
XLA Modules:
  0.0 62.3 jit_solution(13956415917934269404)
XLA Ops:
  0.6 60.1 %shard_map.111 = (bf16[256,128]{1,0:T(8,128)(2,1)}, bf16[32,256]{1,0:T(8,128)(2,1)}, f32[128,128]{1,0:T(8,128)}, f32[1,128]{1,0:T(1,128)}) custom-call(bf16[256,128]{1,0:T(8,128)(2,1)} %feat_h.1, bf16[128,128]{1,0:T(8,128)(2,1)} %weight_h.1, f32[1,128]{1,0:T(1,128)} %bitcast.7, bf16[256,128]{1,0:T(8,128)(2,1)} %cot_h.1, bf16[256,128,128]{2,1,0:T(8,128)(2,1)} %tiles_h.1, ...), custom_call_target="tpu_custom_call" | custom-call | flops 2000000000 | bytes 5000000 | tf_op jit(solution)/shard_map/pallas_call | solution.py:594
  60.7 1.6 %shard_map.112 = (bf16[256,128]{1,0:T(8,128)(2,1)}, bf16[32,256]{1,0:T(8,128)(2,1)}, f32[128,128]{1,0:T(8,128)}, f32[1,128]{1,0:T(1,128)}) custom-call(bf16[256,128]{1,0:T(8,128)(2,1)} %get-tuple-element.12.refs_0_, bf16[32,256]{1,0:T(8,128)(2,1)} %get-tuple-element.13.refs_1_, f32[128,128]{1,0:T(8,128)} %get-tuple-element.14.refs_2_, ...), custom_call_target="tpu_custom_call" | custom-call | tf_op jit(solution)/shard_map/pallas_call | solution.py:652

commit v3 on v2

--- a/solution.py
+++ b/solution.py
@@ -64,6 +64,7 @@
     pt,
     pe,
     pb,
+    pq,
     pf,
     gwb,
     g1,
@@ -92,6 +93,7 @@
     E = 2 * X
     R = T // E
     NEAR = 3
+    WIDE = 5
     me_v = lax.axis_index("vtx")
     me_f = lax.axis_index("feat")
     h = me_v // (Z * X)
@@ -251,7 +253,7 @@
     def far_row(q):
         p = zat(offset(q)) * X + x
         wait_slot(p)
-        for dx in (2, 1, 3):
+        for dx in (1, 3) if q < WIDE else (2, 1, 3):
             slot_copy(p, here(z, xat(dx))).start()
 
     def arrived(q, dx):
@@ -259,6 +261,14 @@
         wait_slot(p)
         forward(p)
 
+    for dx in (1, 3, 2):
+        p = z * X + xat(dx)
+        wait_slot(p)
+        if dx == 2:
+            slot_copy(p, here(zat(2), x)).start()
+            slot_copy(p, here(zat(-2), x)).start()
+        slot_copy(p, here(zat(1), x)).start()
+        slot_copy(p, here(zat(-1), x)).start()
     far_row(3)
     far_row(4)
     first_copy(zat(offset(7)), x).start()
@@ -275,11 +285,6 @@
     far_row(6)
     first_copy(zat(offset(1)), x).start()
     first_copy(zat(offset(2)), x).start()
-    for dx in (1, 3, 2):
-        p = z * X + xat(dx)
-        wait_slot(p)
-        slot_copy(p, here(zat(1), x)).start()
-        slot_copy(p, here(zat(-1), x)).start()
     forward(zat(offset(3)) * X + x)
     forward(zat(offset(4)) * X + x)
     far_row(7)
@@ -380,11 +385,12 @@
         weight_copy(gwb.at[e], g1.at[me_e], gsem.at[0], g1r.at[me_e], target).start()
 
     p_first.wait_recv()
-    pb[...] = pt[c] + pe[0]
-    p_second = exchange(pb, pe.at[1], 4, lo_mate)
+    chip_p = pt[c] + pe[0]
+    pb[...] = chip_p.astype(BF16)
+    p_second = exchange(pb, pq, 4, lo_mate)
     p_second.start()
     p_second.wait_recv()
-    pf[...] = (pb[...] + pe[1]).astype(BF16)
+    pf[...] = (chip_p + pq[...].astype(F32)).astype(BF16)
 
     def own(p):
         s = l * n_half + p
@@ -479,52 +485,48 @@
             def _():
                 fr[h * NS + i] = fs[i, lp]
 
-    def far_x(t, carry):
-        zz = row_to(Z - 1 - t)
-        for dx in (2, 1, 3):
+    def far_x(q):
+        zz = row_to(q)
+        for dx in (1, 3) if q < WIDE else (2, 1, 3):
             put(zz * 3 + dx - 1, own(zz * X + xat(dx)), here(z, xat(dx)))
-        return carry
-
-    def beside_z(t, carry):
-        q, dx = t // 3 + 1, t % 3 + 1
+
+    def beside_z(q, dx):
         zz = row_to(q)
-        put(3 * Z + t, own(zz * X + xat(dx)), here(zz, x))
-        return carry
-
-    def both_ways(t, carry):
-        far_x(t, carry)
-        return beside_z(t, carry)
-
-    first_part = min(Z - NEAR, 6)
-    lax.fori_loop(0, first_part, both_ways, 0)
-    lax.fori_loop(first_part, Z - NEAR, far_x, 0)
-    lax.fori_loop(first_part, 6, beside_z, 0)
+        put(3 * Z + (q - 1) * 3 + dx - 1, own(zz * X + xat(dx)), here(zz, x))
+
+    beside = [(3, 2), (4, 2), (1, 1), (2, 1), (1, 2), (2, 2), (1, 3), (2, 3)]
+    for q in reversed(range(NEAR, Z)):
+        far_x(q)
+        for _ in range(2):
+            if beside:
+                beside_z(*beside.pop(0))
 
     def same_column(q, carry):
         zz = row_to(q)
         deliver(own(zz * X + x), q, zz, x)
         return carry
 
-    lax.fori_loop(0, NEAR, same_column, 0)
     weight_sums_one()
 
-    def this_row_x(dx, carry):
+    def this_row_x(dx):
         value = own(z * X + xat(dx)) + take(3 * Z + dx - 1) + take(3 * Z + 3 + dx - 1)
+        if dx == 2:
+            value = value + take(3 * Z + 6 + dx - 1) + take(3 * Z + 9 + dx - 1)
         deliver(value, Z - 1 + dx, z, xat(dx))
-        return carry
-
-    lax.fori_loop(1, X, this_row_x, 0)
-
-    def far_z(t, carry):
-        q = Z - 1 - t
+
+
+    def far_z(q):
         zz = row_to(q)
         value = own(zz * X + x)
-        for dx in (1, 3, 2):
+        for dx in (1, 3) if q < WIDE else (1, 3, 2):
             value = value + take(zz * 3 + dx - 1)
         deliver(value, q, zz, x)
-        return carry
-
-    lax.fori_loop(0, Z - NEAR, far_z, 0)
+
+    for q in reversed(range(NEAR, Z)):
+        far_z(q)
+    for dx in (1, 3, 2):
+        this_row_x(dx)
+    lax.fori_loop(0, NEAR, same_column, 0)
     weight_sums_two()
 
     def collect(slot, total):
@@ -590,7 +592,7 @@
     n_final = Z + X - 1
     anywhere = pl.BlockSpec(memory_space=pl.ANY)
     vmem = pl.BlockSpec(memory_space=pltpu.VMEM)
-    n_buf = 3 * Z + 6
+    n_buf = 3 * Z + 12
     out, gf, gw, gb = pl.pallas_call(
         functools.partial(kernel, Z),
         out_shape=(
@@ -617,8 +619,9 @@
             pltpu.VMEM((2, T, T), F32),
             pltpu.VMEM((2, T, T), BF16),
             pltpu.VMEM((2, 2, 64, T), F32),
-            pltpu.VMEM((2, 2, 64, T), F32),
-            pltpu.VMEM((2, 64, T), F32),
+            pltpu.VMEM((1, 2, 64, T), F32),
+            pltpu.VMEM((2, 64, T), BF16),
+            pltpu.VMEM((2, 64, T), BF16),
             pltpu.VMEM((2, 64, T), BF16),
             pltpu.VMEM((E, R + 8, T), F32),
             pltpu.VMEM((E, R + 8, T), F32),

time: 62.4 us -> 58.8 us (0.942)
  the two profiles are of different devices: /device:TPU:32 before, /device:TPU:2 now
where the time goes in v3:
time: 58.8 us; the launch traced here: 58.6 us
  Pallas kernels  58 us (99%)
  between operations  0.64 us (1%)
    pallas_call x1, Pallas kernels, on_device(): pl.pallas_call(functools.partial(kernel, Z), out_shape=(jax.ShapeDtypeStr...  56.4 us
    pallas_call x1, Pallas kernels, on_device(): pl.pallas_call(write_out, out_shape=tuple((jax.ShapeDtypeStruct(a.shape,...  1.55 us

profile of v3, /device:TPU:2, one launch (start us, length us, event | category | flops | bytes accessed | tf_op | source)
XLA Modules:
  0.0 58.6 jit_solution(1382962672350291173)
XLA Ops:
  0.6 56.4 %shard_map.111 = (bf16[256,128]{1,0:T(8,128)(2,1)}, bf16[32,256]{1,0:T(8,128)(2,1)}, f32[128,128]{1,0:T(8,128)}, f32[1,128]{1,0:T(1,128)}) custom-call(bf16[256,128]{1,0:T(8,128)(2,1)} %feat_h.1, bf16[128,128]{1,0:T(8,128)(2,1)} %weight_h.1, f32[1,128]{1,0:T(1,128)} %bitcast.7, bf16[256,128]{1,0:T(8,128)(2,1)} %cot_h.1, bf16[256,128,128]{2,1,0:T(8,128)(2,1)} %tiles_h.1, ...), custom_call_target="tpu_custom_call" | custom-call | flops 2000000000 | bytes 5000000 | tf_op jit(solution)/shard_map/pallas_call | solution.py:596
  57.1 1.6 %shard_map.112 = (bf16[256,128]{1,0:T(8,128)(2,1)}, bf16[32,256]{1,0:T(8,128)(2,1)}, f32[128,128]{1,0:T(8,128)}, f32[1,128]{1,0:T(1,128)}) custom-call(bf16[256,128]{1,0:T(8,128)(2,1)} %get-tuple-element.12.refs_0_, bf16[32,256]{1,0:T(8,128)(2,1)} %get-tuple-element.13.refs_1_, f32[128,128]{1,0:T(8,128)} %get-tuple-element.14.refs_2_, ...), custom_call_target="tpu_custom_call" | custom-call | tf_op jit(solution)/shard_map/pallas_call | solution.py:655

commit v4 on v3

--- a/solution.py
+++ b/solution.py
@@ -111,11 +111,13 @@
     core_mate = (me_v, l * 2 + 1 - c)
     lo_mate = (me_v, (1 - l) * 2 + c)
 
+    mirror = 1 - 2 * c
+
     def zat(o):
-        return (z + 2 * Z + o) % Z
+        return (z + 2 * Z + mirror * o) % Z
 
     def xat(o):
-        return (x + X + o) % X
+        return (x + X + mirror * o) % X
 
     def offset(q):
         return ((q + 1) // 2) * (1 - 2 * (q % 2))
@@ -326,15 +328,18 @@
     first.start()
     first.wait_recv()
     sb[...] = acc[c] + ex[0]
-    second = exchange(sb, ex.at[1], 1, lo_mate)
-    second.start()
+    parts = [pl.ds(0, T // 2), pl.ds(T // 2, T // 2)]
+    seconds = [exchange(sb.at[d], ex.at[1, d], 1 + 4 * i, lo_mate) for i, d in enumerate(parts)]
+    thirds = [exchange(axf.at[c, d], axf.at[c, d], 2 + 4 * i, core_mate) for i, d in enumerate(parts)]
+    for copy in seconds:
+        copy.start()
     w_copy.wait()
     bias_copy.wait()
     cot_copy.wait()
-    second.wait_recv()
-    axf[c] = sb[...] + ex[1]
-    third = exchange(axf.at[c], axf.at[c], 2, core_mate)
-    third.start()
+    for d, second, third in zip(parts, seconds, thirds):
+        second.wait_recv()
+        axf[c, d] = sb[d] + ex[1, d]
+        third.start()
 
     def rows_half(r):
         high, low = split(axf[r])
@@ -350,7 +355,8 @@
                 pt[cc, r, ll * 32 : ll * 32 + 32, :] = back[ll * 64 + cc * 32 : ll * 64 + cc * 32 + 32, :]
 
     rows_half(c)
-    exchange(axf.at[c], axf.at[1 - c], 2, core_mate).wait_recv()
+    for i, d in enumerate(parts):
+        exchange(axf.at[c, d], axf.at[1 - c, d], 2 + 4 * i, core_mate).wait_recv()
     rows_half(1 - c)
 
     p_first = exchange(pt.at[1 - c], pe.at[0], 3, core_mate)
@@ -485,21 +491,34 @@
             def _():
                 fr[h * NS + i] = fs[i, lp]
 
-    def far_x(q):
-        zz = row_to(q)
-        for dx in (1, 3) if q < WIDE else (2, 1, 3):
-            put(zz * 3 + dx - 1, own(zz * X + xat(dx)), here(z, xat(dx)))
+    def x_put(zz, dx):
+        put(zz * 3 + dx - 1, own(zz * X + xat(dx)), here(z, xat(dx)))
 
     def beside_z(q, dx):
         zz = row_to(q)
         put(3 * Z + (q - 1) * 3 + dx - 1, own(zz * X + xat(dx)), here(zz, x))
 
-    beside = [(3, 2), (4, 2), (1, 1), (2, 1), (1, 2), (2, 2), (1, 3), (2, 3)]
-    for q in reversed(range(NEAR, Z)):
-        far_x(q)
-        for _ in range(2):
-            if beside:
-                beside_z(*beside.pop(0))
+    def first_sums(t, carry):
+        q = Z - 1 - t
+        zz = row_to(q)
+
+        @pl.when(q >= WIDE)
+        def _():
+            x_put(zz, 2)
+
+        x_put(zz, 1)
+        x_put(zz, 3)
+
+        @pl.when(t < X)
+        def _():
+            q_two = jnp.where(t == 0, 3, 1)
+            dx = jnp.where(t == 0, 2, t)
+            beside_z(q_two, dx)
+            beside_z(q_two + 1, dx)
+
+        return carry
+
+    lax.fori_loop(0, Z - NEAR, first_sums, 0)
 
     def same_column(q, carry):
         zz = row_to(q)
@@ -515,30 +534,35 @@
         deliver(value, Z - 1 + dx, z, xat(dx))
 
 
-    def far_z(q):
+    def far_z(columns, t, carry):
+        q = Z - 1 - t
         zz = row_to(q)
         value = own(zz * X + x)
-        for dx in (1, 3) if q < WIDE else (1, 3, 2):
+        for dx in columns:
             value = value + take(zz * 3 + dx - 1)
         deliver(value, q, zz, x)
-
-    for q in reversed(range(NEAR, Z)):
-        far_z(q)
+        return carry
+
+    lax.fori_loop(0, Z - WIDE, functools.partial(far_z, (1, 3, 2)), 0)
+    lax.fori_loop(Z - WIDE, Z - NEAR, functools.partial(far_z, (1, 3)), 0)
     for dx in (1, 3, 2):
         this_row_x(dx)
     lax.fori_loop(0, NEAR, same_column, 0)
     weight_sums_two()
 
-    def collect(slot, total):
+    def arrive(slot, carry):
         is_self = jnp.logical_and(h == l, slot == h * NS)
 
         @pl.when(jnp.logical_not(is_self))
         def _():
             final_copy(0, 0, slot, core_mate).wait_recv()
 
-        return total + fr[slot].astype(F32)
-
-    both = lax.fori_loop(0, 2 * NS, collect, jnp.zeros((2, 32, T), F32))
+        return carry
+
+    lax.fori_loop(0, 2 * NS, arrive, 0)
+    both = fr[0].astype(F32)
+    for slot in range(1, 2 * NS):
+        both = both + fr[slot].astype(F32)
     for ct in range(2):
         gf_ref[:, ct * T : ct * T + T] = both[ct].astype(BF16)
 
@@ -548,8 +572,8 @@
     gw_ref[...] = g3[...].reshape(T, T)
 
     first.wait_send()
-    second.wait_send()
-    third.wait_send()
+    for copy in seconds + thirds:
+        copy.wait_send()
     p_first.wait_send()
     p_second.wait_send()
     n_sent = Z * X - 1
@@ -635,8 +659,8 @@
             pltpu.SemaphoreType.DMA((8,)),
             pltpu.SemaphoreType.DMA((1,)),
             pltpu.SemaphoreType.DMA((n_half,)),
-            pltpu.SemaphoreType.DMA((5,)),
-            pltpu.SemaphoreType.DMA((5,)),
+            pltpu.SemaphoreType.DMA((7,)),
+            pltpu.SemaphoreType.DMA((7,)),
             pltpu.SemaphoreType.DMA((3,)),
             pltpu.SemaphoreType.DMA((E,)),
             pltpu.SemaphoreType.DMA((Z,)),

time: 58.8 us -> 58.8 us (level)
  no operation moved by 1% of the time
where the time goes in v4:
time: 58.8 us; the launch traced here: 58.7 us
  Pallas kernels  58.1 us (99%)
  between operations  0.64 us (1%)
    pallas_call x1, Pallas kernels, on_device(): pl.pallas_call(functools.partial(kernel, Z), out_shape=(jax.ShapeDtypeStr...  56.5 us
    pallas_call x1, Pallas kernels, on_device(): pl.pallas_call(write_out, out_shape=tuple((jax.ShapeDtypeStruct(a.shape,...  1.55 us

profile of v4, /device:TPU:2, one launch (start us, length us, event | category | flops | bytes accessed | tf_op | source)
XLA Modules:
  0.0 58.7 jit_solution(11208610974577961862)
XLA Ops:
  0.6 56.5 %shard_map.111 = (bf16[256,128]{1,0:T(8,128)(2,1)}, bf16[32,256]{1,0:T(8,128)(2,1)}, f32[128,128]{1,0:T(8,128)}, f32[1,128]{1,0:T(1,128)}) custom-call(bf16[256,128]{1,0:T(8,128)(2,1)} %feat_h.1, bf16[128,128]{1,0:T(8,128)(2,1)} %weight_h.1, f32[1,128]{1,0:T(1,128)} %bitcast.7, bf16[256,128]{1,0:T(8,128)(2,1)} %cot_h.1, bf16[256,128,128]{2,1,0:T(8,128)(2,1)} %tiles_h.1, ...), custom_call_target="tpu_custom_call" | custom-call | flops 2000000000 | bytes 5000000 | tf_op jit(solution)/shard_map/pallas_call | solution.py:620
  57.1 1.6 %shard_map.112 = (bf16[256,128]{1,0:T(8,128)(2,1)}, bf16[32,256]{1,0:T(8,128)(2,1)}, f32[128,128]{1,0:T(8,128)}, f32[1,128]{1,0:T(1,128)}) custom-call(bf16[256,128]{1,0:T(8,128)(2,1)} %get-tuple-element.12.refs_0_, bf16[32,256]{1,0:T(8,128)(2,1)} %get-tuple-element.13.refs_1_, f32[128,128]{1,0:T(8,128)} %get-tuple-element.14.refs_2_, ...), custom_call_target="tpu_custom_call" | custom-call | tf_op jit(solution)/shard_map/pallas_call | solution.py:679
